TPU v7x, 256 devices: a whole 4x4x8 slice. The times are simulated.
256 devices in a mesh: dom: 64 (over z, x, core), sub: 4 (over y).
Axes of the slice: x: 4, y: 4, z: 8, core: 2. Of those that a mesh axis runs over, the one named last changes fastest.
Arguments:
- dofs: float32 [9, 35, 32768], P(None, None, ('dom', 'sub')), may hold values from -6 to 6
- star_matrix: float32 [3, 9, 9, 32768], P(None, None, None, ('dom', 'sub')), may hold values from -2 to 2
- local_solver: float32 [4, 9, 9, 32768], P(None, None, None, ('dom', 'sub')), may hold values from -2 to 2
- neigh_solver: float32 [4, 9, 9, 32768], P(None, None, None, ('dom', 'sub')), may hold values from -2 to 2
- elem_cluster: int32 [32768], P(('dom', 'sub')), may hold values from 0 to 2, as said below
- face_nbr: int32 [4, 32768], P(None, ('dom', 'sub')), may hold values from 0 to 767, as said below
- nbr_face: int32 [4, 32768], P(None, ('dom', 'sub')), may hold values from 0 to 3
- send_table: int32 [768, 5, 4, 32], P(('dom', 'sub')), may hold values from 0 to 128, as said below
- fault_elem: int32 [8192], P(('dom', 'sub')), may hold values from 0 to 127, as said below
- fault_face: int32 [8192], P(('dom', 'sub')), may hold values from 0 to 3
- fault_coef: float32 [9, 8192], P(None, ('dom', 'sub')), may hold values from 0.1 to 0.9
- ck_matrix: float32 [3, 35, 35], replicated, may hold values from -1 to 1
- stiffness: float32 [3, 35, 35], replicated, may hold values from -0.36 to 0.36
- local_flux: float32 [4, 35, 35], replicated, may hold values from -0.36 to 0.36
- neigh_flux: float32 [4, 4, 35, 35], replicated, may hold values from -0.36 to 0.36
- face_trace: float32 [4, 15, 35], replicated, may hold values from -1 to 1
- face_lift: float32 [4, 35, 15], replicated, may hold values from -0.9 to 0.9
Outputs:
- new_dofs: float32 [9, 35, 32768], P(None, None, ('dom', 'sub'))
Inputs may be any that keep to these rules, and one draw needn't show every extreme that they name: `elem_cluster`: every element named in fault_elem is in cluster 0. `face_nbr`: values below 128 name a local element of the same device; a value 128 + q names ghost slot q of the element's own cluster. `send_table`: entry [3 * device + c, r, t, k] is the k-th local element whose cluster-c integral the device sends to the device with dom index greater by r - 2 and sub index t; 128 marks an empty slot. `fault_elem`: the fault slots of one device name distinct local elements; slot k of a device and slot k of the device with the same dom index and sub index XOR 2 are the two sides of one fault face.
All inputs are finite; a program needn't handle non-finite values.
Results may differ from a plain program's by a relative error of at most 0.0001.
Values sent between devices are 32-bit elements; how exact they have to be, the bound alone decides.
A program may use at most 192 MiB of HBM per device.

v0:
```python
import math

import jax
import jax.numpy as jnp
from jax import lax
from jax.sharding import PartitionSpec as P

HIGHEST_PRECISION = lax.Precision.HIGHEST
time_step = 0.25


def passed_along(value, axis, steps):
    count = lax.axis_size(axis)
    first, last = (max(0, -steps), min(count, count - steps))
    return lax.ppermute(value, axis, [(source, source + steps) for source in range(first, last)])


def partner(value, axis, distance):
    mask = 2**distance
    pairs = [(source, source ^ mask) for source in range(lax.axis_size(axis))]
    return lax.ppermute(value, axis, pairs)


def star_sum(matrices, values):
    summed = None
    for outer in range(values.shape[0]):
        for column in range(values.shape[1]):
            term = matrices[outer, :, column, None, :] * values[outer, column][None]
            summed = term if summed is None else summed + term
    return summed


def derive(current, star_matrix, ck_matrix):
    derivs = [current]
    for degree in range(4):
        moved = jnp.einsum("dkl,qle->dqke", ck_matrix, derivs[-1], precision=HIGHEST_PRECISION)
        derivs.append(-star_sum(star_matrix, moved))
    return jnp.stack(derivs)


def integrate(derivs, offset, length):
    summed = jnp.zeros_like(derivs[0])
    for degree in range(5):
        weight = ((offset + length) ** (degree + 1) - offset ** (degree + 1)) / math.factorial(
            degree + 1
        )
        summed = summed + weight[None, None, :] * derivs[degree]
    return summed


def pack(integral, listing):
    padded = jnp.concatenate(
        [integral, jnp.zeros((integral.shape[0], integral.shape[1], 1), jnp.float32)], axis=2
    )
    fetched = jnp.take(padded, listing.reshape(-1), axis=2)
    fetched = fetched.reshape(
        integral.shape[0], integral.shape[1], listing.shape[0], listing.shape[1], listing.shape[2]
    )
    fetched = jnp.transpose(fetched, (2, 3, 0, 1, 4))
    return fetched.reshape(
        listing.shape[0], listing.shape[1], integral.shape[0], integral.shape[1] * listing.shape[2]
    )


def unpack(ghosts, basis_count):
    slot_count = ghosts.shape[3] // basis_count
    opened = ghosts.reshape(
        ghosts.shape[0], ghosts.shape[1], ghosts.shape[2], basis_count, slot_count
    )
    opened = jnp.transpose(opened, (2, 3, 0, 1, 4))
    return opened.reshape(
        ghosts.shape[2], basis_count, ghosts.shape[0] * ghosts.shape[1] * slot_count
    )


def route(buffer):
    shuffled = lax.all_to_all(buffer, "sub", split_axis=2, concat_axis=2, tiled=True)
    pieces = []
    for position in range(5):
        distance = position - 2
        if distance == 0:
            pieces.append(shuffled[:, position])
        else:
            pieces.append(passed_along(shuffled[:, position], "dom", distance))
    return jnp.stack(pieces, axis=1)


def body(
    dofs,
    star_matrix,
    local_solver,
    neigh_solver,
    elem_cluster,
    face_nbr,
    nbr_face,
    send_table,
    fault_elem,
    fault_face,
    fault_coef,
    ck_matrix,
    stiffness,
    local_flux,
    neigh_flux,
    face_trace,
    face_lift,
):
    elements = dofs.shape[2]
    basis_count = dofs.shape[1]
    period = jnp.where(elem_cluster == 0, 1, jnp.where(elem_cluster == 1, 2, 4)).astype(jnp.int32)
    onehot = (fault_elem[:, None] == jnp.arange(elements, dtype=jnp.int32)[None, :]).astype(
        jnp.float32
    )
    fault_traces = face_trace[fault_face]
    fault_lifts = face_lift[fault_face]
    fault_solver = neigh_solver[fault_face, :, :, fault_elem]
    volume_basis = jnp.concatenate([stiffness, local_flux], axis=0)
    volume_star = jnp.concatenate([star_matrix, -local_solver], axis=0)
    face_pick = (nbr_face[:, None, :] == jnp.arange(4, dtype=jnp.int32)[None, :, None]).astype(
        jnp.float32
    )
    self_ids = jnp.arange(elements, dtype=jnp.int32)
    current = dofs
    derivs = None
    for substep in range(4):
        active = substep % period == 0
        renewed = derive(current, star_matrix, ck_matrix)
        if substep == 0:
            derivs = renewed
        else:
            derivs = jnp.where(active[None, None, None, :], renewed, derivs)
        offset = (substep % period).astype(jnp.float32) * time_step
        due_list = [cluster for cluster in range(3) if substep % 2**cluster == 0]
        integrals = {}
        for cluster in due_list:
            integrals[cluster] = integrate(derivs, offset, time_step * 2**cluster)
        arrived = {}
        for cluster in due_list:
            arrived[cluster] = route(pack(integrals[cluster], send_table[cluster])[None])[0]
        blocks = []
        base = jnp.zeros((elements,), jnp.int32)
        start = 0
        for cluster in due_list:
            block = jnp.concatenate(
                [integrals[cluster], unpack(arrived[cluster], basis_count)], axis=2
            )
            blocks.append(block)
            base = jnp.where(elem_cluster == cluster, start, base)
            start = start + block.shape[2]
        combined = jnp.concatenate(blocks, axis=2)
        indices = jnp.concatenate([base[None, :] + face_nbr, (base + self_ids)[None, :]], axis=0)
        fetched = jnp.take(combined, indices.reshape(-1), axis=2)
        fetched = fetched.reshape(combined.shape[0], basis_count, 5, elements)
        own_part = fetched[:, :, 4, :]
        neighbours = fetched[:, :, :4, :]
        moved = jnp.einsum("mkl,qle->mqke", volume_basis, own_part, precision=HIGHEST_PRECISION)
        change = star_sum(volume_star, moved)
        across = jnp.einsum("iokl,qlie->ioqke", neigh_flux, neighbours, precision=HIGHEST_PRECISION)
        lifted_faces = jnp.sum(face_pick[:, :, None, None, :] * across, axis=1)
        change = change - star_sum(neigh_solver, lifted_faces)
        near_side = jnp.einsum(
            "fml,qlf->qmf",
            fault_traces,
            integrals[0][:, :, fault_elem],
            precision=HIGHEST_PRECISION,
        )
        far_side = partner(near_side, "sub", 1)
        fault_state = 0.5 * (near_side + far_side) + fault_coef[:, None, :] * (far_side - near_side)
        lifted = jnp.einsum("flm,qmf->qlf", fault_lifts, fault_state, precision=HIGHEST_PRECISION)
        contrib = jnp.einsum("fpq,qlf->plf", fault_solver, lifted, precision=HIGHEST_PRECISION)
        change = change - jnp.einsum("plf,fe->ple", contrib, onehot, precision=HIGHEST_PRECISION)
        current = current + jnp.where(active[None, None, :], change, 0.0)
    return current


def solution(mesh):
    in_specs = (
        P(None, None, ("dom", "sub")),
        P(None, None, None, ("dom", "sub")),
        P(None, None, None, ("dom", "sub")),
        P(None, None, None, ("dom", "sub")),
        P(("dom", "sub")),
        P(None, ("dom", "sub")),
        P(None, ("dom", "sub")),
        P(("dom", "sub"), None, None, None),
        P(("dom", "sub")),
        P(("dom", "sub")),
        P(None, ("dom", "sub")),
        P(),
        P(),
        P(),
        P(),
        P(),
        P(),
    )
    out_specs = P(None, None, ("dom", "sub"))
    return jax.shard_map(body, mesh=mesh, in_specs=in_specs, out_specs=out_specs, check_vma=False)
```

profile of v0, /device:TPU:129, one launch (start us, length us, event | category | flops | bytes accessed | tf_op | source)
XLA Modules:
  0.0 749.9 jit_solution(2685694387575283742)
XLA Ops:
  20.5 4.2 constant_dynamic-update-slice_fusion.20
  30.4 6.8 broadcast_select_fusion.8
  37.2 5.0 copy.533
  44.3 4.1 reshape.4012
  48.8 4.5 all-to-all-start
  88.0 3.9 collective-permute-start
  125.3 3.7 gather_fusion.10
  129.1 7.0 broadcast_select_fusion.7
  136.1 5.0 copy.535
  143.4 4.2 reshape.4013
  156.3 6.3 all-to-all-done.1
  167.0 4.3 collective-permute-start.5
  178.9 6.6 collective-permute-done.7
  206.1 7.0 broadcast_select_fusion.6
  213.1 5.0 copy.537
  220.4 4.2 reshape.4014
  224.6 3.8 all-to-all-start.2
  274.9 13.5 %copy.391 = f32[9,35,2304]{1,0,2:T(8,128)} copy(f32[9,35,2304]{2,1,0:T(8,128)} %constant_dynamic-update-slice_fusion.15) | data formatting | bytes 5806080 | tf_op jit(solution)/shard_map/concatenate | solution.py:149
  288.4 9.8 %gather_fusion = f32[640,9,35]{2,1,0:T(8,128)} fusion(f32[9,35,2304]{1,0,2:T(8,128)} %copy.391, s32[1024]{0:T(1024)S(1)} %copy-done.293), kind=kCustom, calls=%fused_computation.9 | custom fusion | bytes 1615360 | tf_op jit(solution)/shard_map/jit(_take)/gather | solution.py:151
  298.2 4.6 copy.393
  307.7 4.3 bitcast_dynamic-update-slice_fusion.3
  326.2 6.8 broadcast_select_fusion.5
  333.0 5.0 copy.543
  340.2 4.2 reshape.4015
  344.3 4.5 all-to-all-start.3
  353.1 13.9 %collective-permute-done.17 = f32[9,15,32]{1,0,2:T(8,128)S(1)} collective-permute-done((f32[9,15,32]{1,0,2:T(8,128)S(1)}, f32[9,15,32]{1,0,2:T(8,128)S(1)}, u32[]{:S(2)}, u32[]{:S(2)}) %collective-permute-start.17) | collective-permute-done | bytes 17312 | tf_op jit(solution)/shard_map/ppermute | solution.py:21
  368.8 4.7 collective-permute-start.13
  384.4 6.3 collective-permute-done.16
  402.6 5.1 copy.449
  407.7 6.1 gather_fusion.13
  413.8 4.5 broadcast_select_fusion.4
  434.0 4.5 bitcast_dynamic-update-slice_fusion.1
  451.8 6.8 broadcast_select_fusion.3
  458.6 6.6 copy.550
  465.2 4.0 copy.551
  469.3 4.1 reshape.4016
  480.3 4.7 gather_fusion.15
  489.7 7.0 broadcast_select_fusion.2
  496.7 6.6 copy.552
  503.2 4.0 copy.553
  507.3 4.2 reshape.4017
  512.0 4.2 all-to-all-start.5
  523.7 3.8 collective-permute-start.20
  532.6 6.1 collective-permute-start.22
  558.4 4.6 copy.467
  563.0 4.1 reshape.3787
  583.3 4.6 copy.477
  587.9 4.1 reshape.3789
  593.7 8.7 %copy.478 = f32[9,35,1536]{1,0,2:T(8,128)} copy(f32[9,35,1536]{2,1,0:T(8,128)S(1)} %pad_maximum_fusion) | data formatting | bytes 3870720 | tf_op jit(solution)/shard_map/concatenate | solution.py:149
  602.5 8.1 %gather_fusion.6 = f32[640,9,35]{2,1,0:T(8,128)} fusion(f32[9,35,1536]{1,0,2:T(8,128)} %copy.478, s32[1024]{0:T(1024)} %get-tuple-element.1070), kind=kCustom, calls=%fused_computation.15 | custom fusion | bytes 1615360 | tf_op jit(solution)/shard_map/jit(_take)/gather | solution.py:151
  610.6 4.6 copy.480
  620.1 4.3 bitcast_dynamic-update-slice_fusion
  632.6 3.7 gather_fusion.16
  636.3 6.8 broadcast_select_fusion.1
  643.1 5.0 copy.558
  650.2 4.2 reshape.4018
  654.4 4.6 all-to-all-start.6
  664.7 12.1 %collective-permute-done.31 = f32[9,15,32]{1,0,2:T(8,128)S(1)} collective-permute-done((f32[9,15,32]{1,0,2:T(8,128)S(1)}, f32[9,15,32]{1,0,2:T(8,128)S(1)}, u32[]{:S(2)}, u32[]{:S(2)}) %collective-permute-start.31) | collective-permute-done | bytes 17312 | tf_op jit(solution)/shard_map/ppermute | solution.py:21
  678.6 7.4 collective-permute-start.27
  696.9 6.3 collective-permute-done.30
  715.1 5.3 copy.496
  720.4 6.1 gather_fusion.17
  726.5 4.5 broadcast_select_fusion
  744.6 5.0 fusion.11
  (1179 shorter events, 383.4 us)
Async XLA Ops:
  0.0 304.7 %copy-start = (f32[4,4,35,35]{3,1,2,0:T(4,128)S(1)}, f32[4,4,35,35]{3,1,2,0:T(4,128)}, u32[]{:S(2)}) copy-start(f32[4,4,35,35]{3,1,2,0:T(4,128)} %param.35) | copy-start | bytes 235204
  48.4 36.7 %copy-start.39 = (f32[9,128]{1,0:T(8,128)S(1)}, f32[9,128]{1,0:T(8,128)}, u32[]{:S(2)}) copy-start(f32[9,128]{1,0:T(8,128)} %copy-done.38) | copy-start | bytes 13828
  48.4 36.7 %copy-start.46 = (f32[9,128]{1,0:T(8,128)S(1)}, f32[9,128]{1,0:T(8,128)}, u32[]{:S(2)}) copy-start(f32[9,128]{1,0:T(8,128)} %copy-done.45) | copy-start | bytes 13828
  48.5 36.7 %copy-start.53 = (f32[9,128]{1,0:T(8,128)S(1)}, f32[9,128]{1,0:T(8,128)}, u32[]{:S(2)}) copy-start(f32[9,128]{1,0:T(8,128)} %copy-done.52) | copy-start | bytes 13828
  48.5 36.7 %copy-start.60 = (f32[9,128]{1,0:T(8,128)S(1)}, f32[9,128]{1,0:T(8,128)}, u32[]{:S(2)}) copy-start(f32[9,128]{1,0:T(8,128)} %copy-done.59) | copy-start | bytes 13828
  48.5 36.7 %copy-start.67 = (f32[9,128]{1,0:T(8,128)S(1)}, f32[9,128]{1,0:T(8,128)}, u32[]{:S(2)}) copy-start(f32[9,128]{1,0:T(8,128)} %copy-done.66) | copy-start | bytes 13828
  48.5 36.7 %copy-start.74 = (f32[9,128]{1,0:T(8,128)S(1)}, f32[9,128]{1,0:T(8,128)}, u32[]{:S(2)}) copy-start(f32[9,128]{1,0:T(8,128)} %copy-done.73) | copy-start | bytes 13828
  48.5 36.7 %copy-start.81 = (f32[9,128]{1,0:T(8,128)S(1)}, f32[9,128]{1,0:T(8,128)}, u32[]{:S(2)}) copy-start(f32[9,128]{1,0:T(8,128)} %copy-done.80) | copy-start | bytes 13828
  48.5 36.7 %copy-start.88 = (f32[9,128]{1,0:T(8,128)S(1)}, f32[9,128]{1,0:T(8,128)}, u32[]{:S(2)}) copy-start(f32[9,128]{1,0:T(8,128)} %copy-done.87) | copy-start | bytes 13828
  48.5 36.7 %copy-start.95 = (f32[9,128]{1,0:T(8,128)S(1)}, f32[9,128]{1,0:T(8,128)}, u32[]{:S(2)}) copy-start(f32[9,128]{1,0:T(8,128)} %copy-done.94) | copy-start | bytes 13828
  48.5 36.7 %copy-start.102 = (f32[9,128]{1,0:T(8,128)S(1)}, f32[9,128]{1,0:T(8,128)}, u32[]{:S(2)}) copy-start(f32[9,128]{1,0:T(8,128)} %copy-done.101) | copy-start | bytes 13828
  48.5 36.7 %copy-start.110 = (f32[9,128]{1,0:T(8,128)S(1)}, f32[9,128]{1,0:T(8,128)}, u32[]{:S(2)}) copy-start(f32[9,128]{1,0:T(8,128)} %copy-done.109) | copy-start | bytes 13828
  48.5 36.7 %copy-start.118 = (f32[9,128]{1,0:T(8,128)S(1)}, f32[9,128]{1,0:T(8,128)}, u32[]{:S(2)}) copy-start(f32[9,128]{1,0:T(8,128)} %copy-done.117) | copy-start | bytes 13828
  48.6 36.7 %copy-start.126 = (f32[9,128]{1,0:T(8,128)S(1)}, f32[9,128]{1,0:T(8,128)}, u32[]{:S(2)}) copy-start(f32[9,128]{1,0:T(8,128)} %copy-done.125) | copy-start | bytes 13828
  48.6 36.7 %copy-start.134 = (f32[9,128]{1,0:T(8,128)S(1)}, f32[9,128]{1,0:T(8,128)}, u32[]{:S(2)}) copy-start(f32[9,128]{1,0:T(8,128)} %copy-done.133) | copy-start | bytes 13828
  48.6 36.7 %copy-start.142 = (f32[9,128]{1,0:T(8,128)S(1)}, f32[9,128]{1,0:T(8,128)}, u32[]{:S(2)}) copy-start(f32[9,128]{1,0:T(8,128)} %copy-done.141) | copy-start | bytes 13828
  48.6 36.7 %copy-start.150 = (f32[9,128]{1,0:T(8,128)S(1)}, f32[9,128]{1,0:T(8,128)}, u32[]{:S(2)}) copy-start(f32[9,128]{1,0:T(8,128)} %copy-done.149) | copy-start | bytes 13828
  48.6 36.7 %copy-start.158 = (f32[9,128]{1,0:T(8,128)S(1)}, f32[9,128]{1,0:T(8,128)}, u32[]{:S(2)}) copy-start(f32[9,128]{1,0:T(8,128)} %copy-done.157) | copy-start | bytes 13828
  48.6 36.7 %copy-start.166 = (f32[9,128]{1,0:T(8,128)S(1)}, f32[9,128]{1,0:T(8,128)}, u32[]{:S(2)}) copy-start(f32[9,128]{1,0:T(8,128)} %copy-done.165) | copy-start | bytes 13828
  48.6 36.7 %copy-start.174 = (f32[9,128]{1,0:T(8,128)S(1)}, f32[9,128]{1,0:T(8,128)}, u32[]{:S(2)}) copy-start(f32[9,128]{1,0:T(8,128)} %copy-done.173) | copy-start | bytes 13828
  48.8 38.0 %all-to-all-start = ((f32[1,5,4,9,1120]{4,0,3,1,2:T(1,128)}), f32[1,5,4,9,1120]{4,0,3,1,2:T(1,128)S(1)}, u32[]{:S(2)}, u32[]{:S(2)}) async-start(f32[1,5,4,9,1120]{4,0,3,1,2:T(1,128)} %reshape.4012), calls=%async_computation | async-start | bytes 1658880 | tf_op jit(solution)/shard_map/all_to_all | solution.py:77
  57.3 45.0 %copy-start.11 = (f32[32,15,35]{2,0,1:T(8,128)}, f32[32,15,35]{2,0,1:T(8,128)S(1)}, u32[]{:S(2)}) copy-start(f32[32,15,35]{2,0,1:T(8,128)S(1)} %gather_fusion.2) | copy-start | bytes 201604
  58.7 180.8 %collective-permute-start.12 = (f32[9,15,32]{1,0,2:T(8,128)}, f32[9,15,32]{1,0,2:T(8,128)}, u32[]{:S(2)}, u32[]{:S(2)}) collective-permute-start(f32[9,15,32]{1,0,2:T(8,128)} %convolution_bitcast_fusion.31), channel_id=1, source_target_pairs={{0,2},{1,3},{2,0},{3,1},{4,6},{5,7},{6,4},{7,5},{8,10},{9,11},{10,... | collective-permute-start | bytes 51848 | tf_op jit(solution)/shard_map/ppermute | solution.py:21
  63.6 38.7 %copy-start.345 = (s32[1,128]{1,0:T(1,128)}, s32[1,128]{1,0:T(1,128)S(1)}, u32[]{:S(2)}) copy-start(s32[1,128]{1,0:T(1,128)S(1)} %get-tuple-element.997) | copy-start | bytes 1540
  63.6 38.7 %copy-start.347 = (s32[1,128]{1,0:T(1,128)}, s32[1,128]{1,0:T(1,128)S(1)}, u32[]{:S(2)}) copy-start(s32[1,128]{1,0:T(1,128)S(1)} %get-tuple-element.998) | copy-start | bytes 1540
  88.0 13.0 %collective-permute-start = (f32[1,4,9,1120]{3,0,2,1:T(1,128)S(1)}, f32[1,4,9,1120]{3,0,2,1:T(1,128)}, u32[]{:S(2)}, u32[]{:S(2)}) collective-permute-start(f32[1,4,9,1120]{3,0,2,1:T(1,128)S(1)} %get-tuple-element.311), channel_id=1, source_target_pairs={{8,0},{12,4},{16,8},{20,12},{24,16},{28,20},{32,24},{36,28},{40,32... | collective-permute-start | bytes 483848 | tf_op jit(solution)/shard_map/ppermute | solution.py:15
  92.0 10.3 %collective-permute-start.1 = (f32[1,4,9,1120]{3,0,2,1:T(1,128)S(1)}, f32[1,4,9,1120]{3,0,2,1:T(1,128)}, u32[]{:S(2)}, u32[]{:S(2)}) collective-permute-start(f32[1,4,9,1120]{3,0,2,1:T(1,128)S(1)} %get-tuple-element.310), channel_id=1, source_target_pairs={{4,0},{8,4},{12,8},{16,12},{20,16},{24,20},{28,24},{32,28},{36,32}... | collective-permute-start | bytes 483848 | tf_op jit(solution)/shard_map/ppermute | solution.py:15
  95.7 7.9 %collective-permute-start.2 = (f32[1,4,9,1120]{3,0,2,1:T(1,128)S(1)}, f32[1,4,9,1120]{3,0,2,1:T(1,128)S(1)}, u32[]{:S(2)}, u32[]{:S(2)}) collective-permute-start(f32[1,4,9,1120]{3,0,2,1:T(1,128)S(1)} %get-tuple-element.308), channel_id=1, source_target_pairs={{0,4},{4,8},{8,12},{12,16},{16,20},{20,24},{24,28},{28,32},{32,36}... | collective-permute-start | bytes 483848 | tf_op jit(solution)/shard_map/ppermute | solution.py:15
  97.6 10.8 %collective-permute-start.3 = (f32[1,4,9,1120]{3,0,2,1:T(1,128)}, f32[1,4,9,1120]{3,0,2,1:T(1,128)}, u32[]{:S(2)}, u32[]{:S(2)}) collective-permute-start(f32[1,4,9,1120]{3,0,2,1:T(1,128)} %get-tuple-element.307), channel_id=1, source_target_pairs={{0,8},{4,12},{8,16},{12,20},{16,24},{20,28},{24,32},{28,36},{32,40... | collective-permute-start | bytes 483848 | tf_op jit(solution)/shard_map/ppermute | solution.py:15
  147.6 15.0 %all-to-all-start.1 = ((f32[1,5,4,9,1120]{4,0,3,1,2:T(1,128)}), f32[1,5,4,9,1120]{4,0,3,1,2:T(1,128)S(1)}, u32[]{:S(2)}, u32[]{:S(2)}) async-start(f32[1,5,4,9,1120]{4,0,3,1,2:T(1,128)} %reshape.4013), calls=%async_computation.1 | async-start | bytes 1658880 | tf_op jit(solution)/shard_map/all_to_all | solution.py:77
  163.8 13.1 %collective-permute-start.4 = (f32[1,4,9,1120]{3,0,2,1:T(1,128)S(1)}, f32[1,4,9,1120]{3,0,2,1:T(1,128)S(1)}, u32[]{:S(2)}, u32[]{:S(2)}) collective-permute-start(f32[1,4,9,1120]{3,0,2,1:T(1,128)S(1)} %get-tuple-element.306), channel_id=1, source_target_pairs={{8,0},{12,4},{16,8},{20,12},{24,16},{28,20},{32,24},{36,28},{40,32... | collective-permute-start | bytes 483848 | tf_op jit(solution)/shard_map/ppermute | solution.py:15
  167.0 10.2 %collective-permute-start.5 = (f32[1,4,9,1120]{3,0,2,1:T(1,128)S(1)}, f32[1,4,9,1120]{3,0,2,1:T(1,128)S(1)}, u32[]{:S(2)}, u32[]{:S(2)}) collective-permute-start(f32[1,4,9,1120]{3,0,2,1:T(1,128)S(1)} %get-tuple-element.305), channel_id=1, source_target_pairs={{4,0},{8,4},{12,8},{16,12},{20,16},{24,20},{28,24},{32,28},{36,32}... | collective-permute-start | bytes 483848 | tf_op jit(solution)/shard_map/ppermute | solution.py:15
  171.3 6.3 collective-permute-start.6
  173.9 11.5 %collective-permute-start.7 = (f32[1,4,9,1120]{3,0,2,1:T(1,128)}, f32[1,4,9,1120]{3,0,2,1:T(1,128)}, u32[]{:S(2)}, u32[]{:S(2)}) collective-permute-start(f32[1,4,9,1120]{3,0,2,1:T(1,128)} %get-tuple-element.302), channel_id=1, source_target_pairs={{0,8},{4,12},{8,16},{12,20},{16,24},{20,28},{24,32},{28,36},{32,40... | collective-permute-start | bytes 483848 | tf_op jit(solution)/shard_map/ppermute | solution.py:15
  224.6 16.7 %all-to-all-start.2 = ((f32[1,5,4,9,1120]{4,0,3,1,2:T(1,128)}), f32[1,5,4,9,1120]{4,0,3,1,2:T(1,128)S(1)}, u32[]{:S(2)}, u32[]{:S(2)}) async-start(f32[1,5,4,9,1120]{4,0,3,1,2:T(1,128)} %reshape.4014), calls=%async_computation.2 | async-start | bytes 1658880 | tf_op jit(solution)/shard_map/all_to_all | solution.py:77
  242.5 12.3 %collective-permute-start.8 = (f32[1,4,9,1120]{3,0,2,1:T(1,128)S(1)}, f32[1,4,9,1120]{3,0,2,1:T(1,128)S(1)}, u32[]{:S(2)}, u32[]{:S(2)}) collective-permute-start(f32[1,4,9,1120]{3,0,2,1:T(1,128)S(1)} %get-tuple-element.301), channel_id=1, source_target_pairs={{8,0},{12,4},{16,8},{20,12},{24,16},{28,20},{32,24},{36,28},{40,32... | collective-permute-start | bytes 483848 | tf_op jit(solution)/shard_map/ppermute | solution.py:15
  244.4 10.7 %collective-permute-start.9 = (f32[1,4,9,1120]{3,0,2,1:T(1,128)S(1)}, f32[1,4,9,1120]{3,0,2,1:T(1,128)}, u32[]{:S(2)}, u32[]{:S(2)}) collective-permute-start(f32[1,4,9,1120]{3,0,2,1:T(1,128)S(1)} %get-tuple-element.300), channel_id=1, source_target_pairs={{4,0},{8,4},{12,8},{16,12},{20,16},{24,20},{28,24},{32,28},{36,32}... | collective-permute-start | bytes 483848 | tf_op jit(solution)/shard_map/ppermute | solution.py:15
  247.1 9.2 %collective-permute-start.10 = (f32[1,4,9,1120]{3,0,2,1:T(1,128)}, f32[1,4,9,1120]{3,0,2,1:T(1,128)}, u32[]{:S(2)}, u32[]{:S(2)}) collective-permute-start(f32[1,4,9,1120]{3,0,2,1:T(1,128)} %get-tuple-element.298), channel_id=1, source_target_pairs={{0,4},{4,8},{8,12},{12,16},{16,20},{20,24},{24,28},{28,32},{32,36}... | collective-permute-start | bytes 483848 | tf_op jit(solution)/shard_map/ppermute | solution.py:15
  250.7 10.6 %collective-permute-start.11 = (f32[1,4,9,1120]{3,0,2,1:T(1,128)S(1)}, f32[1,4,9,1120]{3,0,2,1:T(1,128)}, u32[]{:S(2)}, u32[]{:S(2)}) collective-permute-start(f32[1,4,9,1120]{3,0,2,1:T(1,128)S(1)} %get-tuple-element.297), channel_id=1, source_target_pairs={{0,8},{4,12},{8,16},{12,20},{16,24},{20,28},{24,32},{28,36},{32,40... | collective-permute-start | bytes 483848 | tf_op jit(solution)/shard_map/ppermute | solution.py:15
  344.3 36.7 %copy-start.16 = (f32[32,9,9]{2,1,0:T(8,128)S(1)}, f32[32,9,9]{2,1,0:T(8,128)}, u32[]{:S(2)}) copy-start(f32[32,9,9]{2,1,0:T(8,128)} %copy-done.15) | copy-start | bytes 31108
  344.3 23.2 %all-to-all-start.3 = ((f32[1,5,4,9,1120]{4,0,3,1,2:T(1,128)}), f32[1,5,4,9,1120]{4,0,3,1,2:T(1,128)S(1)}, u32[]{:S(2)}, u32[]{:S(2)}) async-start(f32[1,5,4,9,1120]{4,0,3,1,2:T(1,128)} %reshape.4015), calls=%async_computation.3 | async-start | bytes 1658880 | tf_op jit(solution)/shard_map/all_to_all | solution.py:77
  349.5 17.5 %collective-permute-start.17 = (f32[9,15,32]{1,0,2:T(8,128)S(1)}, f32[9,15,32]{1,0,2:T(8,128)S(1)}, u32[]{:S(2)}, u32[]{:S(2)}) collective-permute-start(f32[9,15,32]{1,0,2:T(8,128)S(1)} %convolution_bitcast_fusion.28), channel_id=1, source_target_pairs={{0,2},{1,3},{2,0},{3,1},{4,6},{5,7},{6,4},{7,5},{8,10},{9,11},{10,... | collective-permute-start | bytes 51848 | tf_op jit(solution)/shard_map/ppermute | solution.py:21
  368.8 13.7 %collective-permute-start.13 = (f32[1,4,9,1120]{3,0,2,1:T(1,128)S(1)}, f32[1,4,9,1120]{3,0,2,1:T(1,128)S(1)}, u32[]{:S(2)}, u32[]{:S(2)}) collective-permute-start(f32[1,4,9,1120]{3,0,2,1:T(1,128)S(1)} %get-tuple-element.296), channel_id=1, source_target_pairs={{8,0},{12,4},{16,8},{20,12},{24,16},{28,20},{32,24},{36,28},{40,32... | collective-permute-start | bytes 483848 | tf_op jit(solution)/shard_map/ppermute | solution.py:15
  373.5 9.3 %collective-permute-start.14 = (f32[1,4,9,1120]{3,0,2,1:T(1,128)S(1)}, f32[1,4,9,1120]{3,0,2,1:T(1,128)S(1)}, u32[]{:S(2)}, u32[]{:S(2)}) collective-permute-start(f32[1,4,9,1120]{3,0,2,1:T(1,128)S(1)} %get-tuple-element.295), channel_id=1, source_target_pairs={{4,0},{8,4},{12,8},{16,12},{20,16},{24,20},{28,24},{32,28},{36,32}... | collective-permute-start | bytes 483848 | tf_op jit(solution)/shard_map/ppermute | solution.py:15
  376.1 7.0 collective-permute-start.15
  379.1 11.6 %collective-permute-start.16 = (f32[1,4,9,1120]{3,0,2,1:T(1,128)}, f32[1,4,9,1120]{3,0,2,1:T(1,128)}, u32[]{:S(2)}, u32[]{:S(2)}) collective-permute-start(f32[1,4,9,1120]{3,0,2,1:T(1,128)} %get-tuple-element.292), channel_id=1, source_target_pairs={{0,8},{4,12},{8,16},{12,20},{16,24},{20,28},{24,32},{28,36},{32,40... | collective-permute-start | bytes 483848 | tf_op jit(solution)/shard_map/ppermute | solution.py:15
  473.4 38.7 %all-to-all-start.4 = ((f32[1,5,4,9,1120]{4,0,3,1,2:T(1,128)}), f32[1,5,4,9,1120]{4,0,3,1,2:T(1,128)S(1)}, u32[]{:S(2)}, u32[]{:S(2)}) async-start(f32[1,5,4,9,1120]{4,0,3,1,2:T(1,128)} %reshape.4016), calls=%async_computation.4 | async-start | bytes 1658880 | tf_op jit(solution)/shard_map/all_to_all | solution.py:77
  486.6 24.8 %collective-permute-start.26 = (f32[9,15,32]{1,0,2:T(8,128)S(1)}, f32[9,15,32]{1,0,2:T(8,128)S(1)}, u32[]{:S(2)}, u32[]{:S(2)}) collective-permute-start(f32[9,15,32]{1,0,2:T(8,128)S(1)} %convolution_bitcast_fusion.25), channel_id=1, source_target_pairs={{0,2},{1,3},{2,0},{3,1},{4,6},{5,7},{6,4},{7,5},{8,10},{9,11},{10,... | collective-permute-start | bytes 51848 | tf_op jit(solution)/shard_map/ppermute | solution.py:21
  512.0 18.0 %all-to-all-start.5 = ((f32[1,5,4,9,1120]{4,0,3,1,2:T(1,128)}), f32[1,5,4,9,1120]{4,0,3,1,2:T(1,128)}, u32[]{:S(2)}, u32[]{:S(2)}) async-start(f32[1,5,4,9,1120]{4,0,3,1,2:T(1,128)} %reshape.4017), calls=%async_computation.5 | async-start | bytes 1658880 | tf_op jit(solution)/shard_map/all_to_all | solution.py:77
  518.6 20.4 %collective-permute-start.18 = (f32[1,4,9,1120]{3,0,2,1:T(1,128)}, f32[1,4,9,1120]{3,0,2,1:T(1,128)S(1)}, u32[]{:S(2)}, u32[]{:S(2)}) collective-permute-start(f32[1,4,9,1120]{3,0,2,1:T(1,128)} %get-tuple-element.286), channel_id=1, source_target_pairs={{8,0},{12,4},{16,8},{20,12},{24,16},{28,20},{32,24},{36,28},{40,32... | collective-permute-start | bytes 483848 | tf_op jit(solution)/shard_map/ppermute | solution.py:15
  520.6 23.3 %collective-permute-start.19 = (f32[1,4,9,1120]{3,0,2,1:T(1,128)}, f32[1,4,9,1120]{3,0,2,1:T(1,128)}, u32[]{:S(2)}, u32[]{:S(2)}) collective-permute-start(f32[1,4,9,1120]{3,0,2,1:T(1,128)} %get-tuple-element.285), channel_id=1, source_target_pairs={{4,0},{8,4},{12,8},{16,12},{20,16},{24,20},{28,24},{32,28},{36,32}... | collective-permute-start | bytes 483848 | tf_op jit(solution)/shard_map/ppermute | solution.py:15
  523.7 28.4 %collective-permute-start.20 = (f32[1,4,9,1120]{3,0,2,1:T(1,128)}, f32[1,4,9,1120]{3,0,2,1:T(1,128)}, u32[]{:S(2)}, u32[]{:S(2)}) collective-permute-start(f32[1,4,9,1120]{3,0,2,1:T(1,128)} %get-tuple-element.283), channel_id=1, source_target_pairs={{0,4},{4,8},{8,12},{12,16},{16,20},{20,24},{24,28},{28,32},{32,36}... | collective-permute-start | bytes 483848 | tf_op jit(solution)/shard_map/ppermute | solution.py:15
  527.5 28.7 %collective-permute-start.21 = (f32[1,4,9,1120]{3,0,2,1:T(1,128)}, f32[1,4,9,1120]{3,0,2,1:T(1,128)}, u32[]{:S(2)}, u32[]{:S(2)}) collective-permute-start(f32[1,4,9,1120]{3,0,2,1:T(1,128)} %get-tuple-element.282), channel_id=1, source_target_pairs={{0,8},{4,12},{8,16},{12,20},{16,24},{20,28},{24,32},{28,36},{32,40... | collective-permute-start | bytes 483848 | tf_op jit(solution)/shard_map/ppermute | solution.py:15
  532.6 34.4 %collective-permute-start.22 = (f32[1,4,9,1120]{3,0,2,1:T(1,128)}, f32[1,4,9,1120]{3,0,2,1:T(1,128)}, u32[]{:S(2)}, u32[]{:S(2)}) collective-permute-start(f32[1,4,9,1120]{3,0,2,1:T(1,128)} %get-tuple-element.291), channel_id=1, source_target_pairs={{8,0},{12,4},{16,8},{20,12},{24,16},{28,20},{32,24},{36,28},{40,32... | collective-permute-start | bytes 483848 | tf_op jit(solution)/shard_map/ppermute | solution.py:15
  539.0 29.3 %collective-permute-start.23 = (f32[1,4,9,1120]{3,0,2,1:T(1,128)}, f32[1,4,9,1120]{3,0,2,1:T(1,128)}, u32[]{:S(2)}, u32[]{:S(2)}) collective-permute-start(f32[1,4,9,1120]{3,0,2,1:T(1,128)} %get-tuple-element.290), channel_id=1, source_target_pairs={{4,0},{8,4},{12,8},{16,12},{20,16},{24,20},{28,24},{32,28},{36,32}... | collective-permute-start | bytes 483848 | tf_op jit(solution)/shard_map/ppermute | solution.py:15
  543.8 27.3 %collective-permute-start.24 = (f32[1,4,9,1120]{3,0,2,1:T(1,128)}, f32[1,4,9,1120]{3,0,2,1:T(1,128)}, u32[]{:S(2)}, u32[]{:S(2)}) collective-permute-start(f32[1,4,9,1120]{3,0,2,1:T(1,128)} %get-tuple-element.288), channel_id=1, source_target_pairs={{0,4},{4,8},{8,12},{12,16},{16,20},{20,24},{24,28},{28,32},{32,36}... | collective-permute-start | bytes 483848 | tf_op jit(solution)/shard_map/ppermute | solution.py:15
  552.1 23.6 %collective-permute-start.25 = (f32[1,4,9,1120]{3,0,2,1:T(1,128)}, f32[1,4,9,1120]{3,0,2,1:T(1,128)}, u32[]{:S(2)}, u32[]{:S(2)}) collective-permute-start(f32[1,4,9,1120]{3,0,2,1:T(1,128)} %get-tuple-element.287), channel_id=1, source_target_pairs={{0,8},{4,12},{8,16},{12,20},{16,24},{20,28},{24,32},{28,36},{32,40... | collective-permute-start | bytes 483848 | tf_op jit(solution)/shard_map/ppermute | solution.py:15
  654.4 39.1 %copy-start.18 = (f32[32,9,9]{2,1,0:T(8,128)S(1)}, f32[32,9,9]{2,1,0:T(8,128)}, u32[]{:S(2)}) copy-start(f32[32,9,9]{2,1,0:T(8,128)} %copy-done.15) | copy-start | bytes 31108
  654.4 23.0 %all-to-all-start.6 = ((f32[1,5,4,9,1120]{4,0,3,1,2:T(1,128)}), f32[1,5,4,9,1120]{4,0,3,1,2:T(1,128)S(1)}, u32[]{:S(2)}, u32[]{:S(2)}) async-start(f32[1,5,4,9,1120]{4,0,3,1,2:T(1,128)} %reshape.4018), calls=%async_computation.6 | async-start | bytes 1658880 | tf_op jit(solution)/shard_map/all_to_all | solution.py:77
  661.6 15.2 %collective-permute-start.31 = (f32[9,15,32]{1,0,2:T(8,128)S(1)}, f32[9,15,32]{1,0,2:T(8,128)S(1)}, u32[]{:S(2)}, u32[]{:S(2)}) collective-permute-start(f32[9,15,32]{1,0,2:T(8,128)S(1)} %convolution_bitcast_fusion.22), channel_id=1, source_target_pairs={{0,2},{1,3},{2,0},{3,1},{4,6},{5,7},{6,4},{7,5},{8,10},{9,11},{10,... | collective-permute-start | bytes 51848 | tf_op jit(solution)/shard_map/ppermute | solution.py:21
  678.6 16.3 %collective-permute-start.27 = (f32[1,4,9,1120]{3,0,2,1:T(1,128)S(1)}, f32[1,4,9,1120]{3,0,2,1:T(1,128)S(1)}, u32[]{:S(2)}, u32[]{:S(2)}) collective-permute-start(f32[1,4,9,1120]{3,0,2,1:T(1,128)S(1)} %get-tuple-element.281), channel_id=1, source_target_pairs={{8,0},{12,4},{16,8},{20,12},{24,16},{28,20},{32,24},{36,28},{40,32... | collective-permute-start | bytes 483848 | tf_op jit(solution)/shard_map/ppermute | solution.py:15
  686.0 9.2 %collective-permute-start.28 = (f32[1,4,9,1120]{3,0,2,1:T(1,128)S(1)}, f32[1,4,9,1120]{3,0,2,1:T(1,128)S(1)}, u32[]{:S(2)}, u32[]{:S(2)}) collective-permute-start(f32[1,4,9,1120]{3,0,2,1:T(1,128)S(1)} %get-tuple-element.280), channel_id=1, source_target_pairs={{4,0},{8,4},{12,8},{16,12},{20,16},{24,20},{28,24},{32,28},{36,32}... | collective-permute-start | bytes 483848 | tf_op jit(solution)/shard_map/ppermute | solution.py:15
  688.6 7.0 collective-permute-start.29
  691.6 11.6 %collective-permute-start.30 = (f32[1,4,9,1120]{3,0,2,1:T(1,128)}, f32[1,4,9,1120]{3,0,2,1:T(1,128)}, u32[]{:S(2)}, u32[]{:S(2)}) collective-permute-start(f32[1,4,9,1120]{3,0,2,1:T(1,128)} %get-tuple-element.277), channel_id=1, source_target_pairs={{0,8},{4,12},{8,16},{12,20},{16,24},{20,28},{24,32},{28,36},{32,40... | collective-permute-start | bytes 483848 | tf_op jit(solution)/shard_map/ppermute | solution.py:15
  (353 other events, 3055.9 us)
where the time goes:
time: 763 us; the launch traced here: 750 us
  local copies, waits for them, and re-layouts  386 us (51%)
  starting transfers between devices  128 us (17%)
  other arithmetic  106 us (14%)
  matrix products  65.9 us (9%)
  waiting for transfers between devices  56.9 us (7%)
    ppermute x28, starting transfers between devices, passed_along(): lax.ppermute(value, axis, [(source, source + steps) for source in range(f...  86.6 us
    unnamed x803, local copies, waits for them, and re-layouts  55.8 us
    select_n x10, other arithmetic, pack(): fetched = jnp.take(padded, listing.reshape(-1), axis=2)  48.8 us
    another operation x14, local copies, waits for them, and re-layouts, body(): pack(integrals[cluster], send_table[cluster])[None]  47.5 us
    gather x6, local copies, waits for them, and re-layouts, body(): fetched = jnp.take(combined, indices.reshape(-1), axis=2)  39.4 us
    reshape x7, local copies, waits for them, and re-layouts, pack(): fetched.reshape(integral.shape[0], integral.shape[1], listing.shape[0], l...  38.1 us
    all_to_all x7, starting transfers between devices, route(): lax.all_to_all(buffer, 'sub', split_axis=2, concat_axis=2, tiled=True)  28.9 us
    gather x7, local copies, waits for them, and re-layouts, pack(): fetched = jnp.take(padded, listing.reshape(-1), axis=2)  27.1 us
  transfers between devices with their start and end apart: 39, of which 8 were waited for; matrix products, arithmetic and copies ran while one was open for 29% of the time, Pallas kernels for 0%

commit v1 on v0

v1 whole, which is shorter than its diff:
```python
import functools

import jax
import jax.numpy as jnp
from jax import lax
from jax.experimental import pallas as pl
from jax.experimental.pallas import tpu as pltpu
from jax.sharding import PartitionSpec as P

MESH = pl.DeviceIdType.MESH
F32 = jnp.float32
BF16 = jnp.bfloat16
Q = 9
B = 35
KP = 40
E = 128
W = Q * E
FB = 15
NF = 32
SLOT = 32
REACH = 5
N_SUB = 4
PEERS = REACH * N_SUB
ROWS = 320
PIECE = ROWS // N_SUB
TAIL = Q * 32
STEP = 0.25
ROUTES = {(0, 0): 0, (0, 1): 1, (0, 2): 2, (1, 0): 3, (2, 0): 4, (2, 1): 5, (3, 0): 6}


def halves(value):
    high = value.astype(BF16).astype(F32)
    return high, value - high


def stacked(value):
    high, low = halves(value)
    return jnp.concatenate([high, low, high, jnp.zeros((8, E), F32)], axis=0).astype(BF16)


def weights(matrix, width):
    high, low = halves(matrix)
    return high + pltpu.roll(high, width, 1) + pltpu.roll(low, 2 * width, 1)


def dot(left, right):
    return jnp.dot(left, right, preferred_element_type=F32)


def lanes(index, count=1):
    return pl.ds(pl.multiple_of(index * E, E), count * E)


def exchanged(parts, low_half, even):
    mixed = [None] * 4
    for g in range(2):
        mixed[g] = jnp.where(low_half, parts[g], pltpu.roll(parts[g + 2], 64, 1))
        mixed[g + 2] = jnp.where(low_half, pltpu.roll(parts[g], 64, 1), parts[g + 2])
    out = [None] * 4
    for g in (0, 2):
        out[g] = jnp.where(even, mixed[g], pltpu.roll(mixed[g + 1], 32, 1))
        out[g + 1] = jnp.where(even, pltpu.roll(mixed[g], 96, 1), mixed[g + 1])
    return out


def kernel(
    n_dom,
    dofs,
    star,
    lsol,
    nsol,
    ecl,
    fnbr,
    nface,
    stab,
    felem,
    fface,
    fcoef,
    ck,
    stiff,
    lflux,
    nflux,
    ftrace,
    flift,
    out,
    base,
    cur,
    integ,
    x_der,
    x_own,
    x_nbr,
    x_state,
    moved,
    across,
    lifted,
    lift,
    near,
    far,
    fsend,
    frecv,
    comp,
    comp_h,
    got,
    ghost,
    packed,
    pick,
    pick_send,
    pick_f,
    pick_ft,
    a_ck,
    a_vol,
    a_nf,
    a_tr,
    a_li,
    wide,
    tab,
    fer,
    cfs,
    cfe,
    wt,
    send,
    recv,
    send_sem,
    recv_sem,
    fsend_sem,
    frecv_sem,
):
    dom = lax.axis_index("dom")
    sub = lax.axis_index("sub")

    def out_peer(idx):
        r, t = idx // N_SUB, idx % N_SUB
        peer = dom + r - 2
        valid = (peer >= 0) & (peer < n_dom) & jnp.logical_not((r == 2) & (t == sub))
        return peer, t, valid

    def in_peer(idx):
        r, t = idx // N_SUB, idx % N_SUB
        peer = dom - r + 2
        valid = (peer >= 0) & (peer < n_dom) & jnp.logical_not((r == 2) & (t == sub))
        return peer, t, valid

    barrier = pltpu.get_barrier_semaphore()

    @pl.loop(0, PEERS)
    def _(idx):
        peer, t, valid = out_peer(idx)

        @pl.when(valid)
        def _():
            pl.semaphore_signal(barrier, inc=1, device_id=(peer, t), device_id_type=MESH)

    lane = lax.broadcasted_iota(jnp.int32, (16, E), 1)
    low_half = lane < 64
    even = (lane // 32) % 2 == 0
    element_rows = lax.broadcasted_iota(jnp.int32, (E, E), 0)

    base[...] = jnp.zeros((Q, KP, E), F32)
    base[:, :B, :] = dofs[...]
    cur[...] = base[...]
    wide[...] = jnp.zeros(wide.shape, F32)
    for d in range(3):
        wide[d, :B, :B] = ck[d]
    a_ck[...] = jnp.concatenate(
        [weights(wide[d], KP) for d in range(3)] + [jnp.zeros((8, E), F32)], axis=0
    ).astype(BF16)
    cluster_of = ecl[...]

    def star_terms(acc, coef, first, rows, group, sign):
        for q in range(Q):
            value = moved[rows : rows + KP, q * E : (q + 1) * E]
            for pp in range(3):
                term = coef[first, group * 3 + pp, q : q + 1, :] * value
                if acc[pp] is None:
                    acc[pp] = term if sign > 0 else -term
                else:
                    acc[pp] = acc[pp] + term if sign > 0 else acc[pp] - term
        return acc

    def derive(s, due):
        if s > 0:
            keep = cluster_of == 0
            if s % 2 == 0:
                keep = cluster_of <= 1
            for q in range(Q):
                base[q] = jnp.where(keep, cur[q], base[q])
        offset = jnp.where(
            cluster_of == 0, 0.0, jnp.where(cluster_of == 1, (s % 2) * STEP, (s % 4) * STEP)
        ).astype(F32)
        for c in due:
            end = offset + STEP * 2**c
            upper, lower, factor = end, offset, 1.0
            for j in range(5):
                factor = factor * (j + 1)
                wt[5 * c + j : 5 * c + j + 1, :] = (upper - lower) * (1.0 / factor)
                upper, lower = upper * end, lower * offset
        for q in range(Q):
            value = base[q]
            x_der[:, q * E : (q + 1) * E] = stacked(value)
            for c in due:
                integ[c, q] = wt[5 * c : 5 * c + 1, :] * value

        @pl.loop(0, 4)
        def _(j):
            moved[0:E, :] = dot(a_ck[...], x_der[...])

            @pl.loop(0, 3)
            def _(group):
                acc = [None, None, None]
                for d in range(3):
                    acc = star_terms(acc, star, d, d * KP, group, -1)
                for pp in range(3):
                    p = group * 3 + pp
                    x_der[:, lanes(p)] = stacked(acc[pp])
                    for c in due:
                        integ[c, p] = integ[c, p] + wt[pl.ds(5 * c + 1 + j, 1), :] * acc[pp]

    def pack(c, route):
        for q in range(Q):
            comp[32 * q : 32 * q + 32, :] = integ[c, q, 0:32, :]
        for q in range(Q):
            comp[TAIL + 3 * q : TAIL + 3 * q + 8, :] = integ[c, q, 32:40, :]
        high, low = halves(comp[...])
        comp_h[c] = jnp.concatenate([high, low], axis=1).astype(BF16)
        picks = pick_send[c]
        packed[...] = dot(comp_h[c], jnp.concatenate([picks, picks], axis=0))

        @pl.loop(0, REACH)
        def _(r):
            for chunk in range(PIECE // 16):
                parts = [
                    packed[PIECE * g + 16 * chunk : PIECE * g + 16 * chunk + 16, lanes(r)]
                    for g in range(4)
                ]
                for t, part in enumerate(exchanged(parts, low_half, even)):
                    send[route, r * N_SUB + t, 16 * chunk : 16 * chunk + 16, :] = part

        recv[route, 2 * N_SUB + sub] = send[route, 2 * N_SUB + sub]

    def ghost_copy(route, out_idx, landing, peer, t):
        return pltpu.make_async_remote_copy(
            src_ref=send.at[route, out_idx],
            dst_ref=recv.at[route, landing],
            send_sem=send_sem.at[route, out_idx],
            recv_sem=recv_sem.at[route, landing],
            device_id=(peer, t),
            device_id_type=MESH,
        )

    def send_route(route):
        @pl.loop(0, PEERS)
        def _(idx):
            peer, t, valid = out_peer(idx)

            @pl.when(valid)
            def _():
                ghost_copy(route, idx, (idx // N_SUB) * N_SUB + sub, peer, t).start()

    def local_gather(c, first):
        picks = pick[c, 0]
        value = dot(comp_h[c], jnp.concatenate([picks, picks], axis=0))
        if first:
            got[...] = value
        else:
            got[...] += value

    def ghost_gather(c, route):
        @pl.loop(0, REACH)
        def _(r):
            for t in range(N_SUB):
                idx = r * N_SUB + t
                peer, _, valid = in_peer(idx)

                @pl.when(valid)
                def _():
                    ghost_copy(route, idx, idx, peer, t).wait_recv()

            for chunk in range(PIECE // 16):
                parts = [
                    recv[route, r * N_SUB + t, 16 * chunk : 16 * chunk + 16, :]
                    for t in range(N_SUB)
                ]
                for g, part in enumerate(exchanged(parts, low_half, even)):
                    start = PIECE * g + 16 * chunk
                    high, low = halves(part)
                    ghost[start : start + 16, 0:E] = high.astype(BF16)
                    ghost[start : start + 16, E : 2 * E] = low.astype(BF16)
            picks = pick[c, 1 + r]
            got[...] += dot(ghost[...], jnp.concatenate([picks, picks], axis=0))

    def own_columns(due):
        for q in range(Q):
            own = None
            for c in due:
                part = jnp.where(cluster_of == c, integ[c, q], 0.0)
                own = part if own is None else own + part
            x_own[:, q * E : (q + 1) * E] = stacked(own)

    def far_copy(s):
        return pltpu.make_async_remote_copy(
            src_ref=fsend.at[s],
            dst_ref=frecv.at[s],
            send_sem=fsend_sem.at[s],
            recv_sem=frecv_sem.at[s],
            device_id=(dom, (sub + 2) % N_SUB),
            device_id_type=MESH,
        )

    def send_near(s):
        moved[0:64, :] = dot(a_tr[...], x_own[...])
        marks = [cfe[16:17, :] == (i + 1.0) for i in range(4)]
        for q in range(Q):
            value = jnp.zeros((16, E), F32)
            for i in range(4):
                part = moved[16 * i : 16 * i + 16, q * E : (q + 1) * E]
                value = value + jnp.where(marks[i], part, 0.0)
            near[16 * q : 16 * q + 16, :] = value
        folded = None
        for g in range(4):
            high, low = halves(near[KP * g : KP * g + KP, :])
            part = dot(jnp.concatenate([high, low], axis=0).astype(BF16), pick_f[g])
            part = part[0:KP] + part[KP : 2 * KP]
            folded = part if folded is None else folded + part
        fsend[s] = folded
        far_copy(s).start()

    def volume():
        moved[...] = dot(a_vol[...], x_own[...])

        @pl.loop(0, 3)
        def _(group):
            acc = [cur[group * 3 + pp] for pp in range(3)]
            for d in range(3):
                acc = star_terms(acc, star, d, d * KP, group, 1)
            for i in range(4):
                acc = star_terms(acc, lsol, i, (3 + i) * KP, group, -1)
            for pp in range(3):
                cur[group * 3 + pp] = acc[pp]

    def fault(s):
        far_copy(s).wait_recv()
        high, low = halves(frecv[s])
        value = jnp.concatenate([high, low], axis=0).astype(BF16)
        for g in range(4):
            part = dot(value, pick_ft[g])
            far[KP * g : KP * g + KP, :] = part[0:KP] + part[KP : 2 * KP]
        for q in range(Q):
            mine, other = near[16 * q : 16 * q + 16, :], far[16 * q : 16 * q + 16, :]
            state = 0.5 * (mine + other) + cfe[q : q + 1, :] * (other - mine)
            high, low = halves(state)
            cols = slice(q * E, (q + 1) * E)
            x_state[0:48, cols] = jnp.concatenate([high, low, high], axis=0).astype(BF16)
        lift[...] = dot(a_li[...], x_state[...])

    def neighbours():
        @pl.loop(0, 4)
        def _(i):
            for q in range(Q):
                main = got[32 * q : 32 * q + 32, lanes(i)]
                tail = got[TAIL + 3 * q : TAIL + 3 * q + 8, lanes(i)]
                x_nbr[:, q * E : (q + 1) * E] = stacked(jnp.concatenate([main, tail], axis=0))
            across[...] = dot(a_nf[i], x_nbr[...])
            which = nface[pl.ds(i, 1), :]
            mark = cfe[16:17, :] == (i + 1).astype(F32)
            at = pl.multiple_of(i * KP, 8)
            for q in range(Q):
                cols = slice(q * E, (q + 1) * E)
                value = across[3 * KP : 4 * KP, cols]
                for j in range(2, -1, -1):
                    value = jnp.where(which == j, across[j * KP : (j + 1) * KP, cols], value)
                lifted[pl.ds(at, KP), cols] = value + jnp.where(mark, lift[pl.ds(at, KP), cols], 0.0)

        @pl.loop(0, 3)
        def _(group):
            acc = [cur[group * 3 + pp] for pp in range(3)]
            for i in range(4):
                for q in range(Q):
                    value = lifted[i * KP : (i + 1) * KP, q * E : (q + 1) * E]
                    for pp in range(3):
                        acc[pp] = acc[pp] - nsol[i, group * 3 + pp, q : q + 1, :] * value
            for pp in range(3):
                cur[group * 3 + pp] = acc[pp]

    def prepare_pick_send(c):
        for r in range(REACH):
            row = tab[c, r : r + 1, :]
            pick_send[c, :, r * E : (r + 1) * E] = jnp.where(element_rows == row, 1.0, 0.0).astype(BF16)

    def prepare_pick(c):
        @pl.loop(0, 1 + REACH)
        def _(g):
            for i in range(4):
                row = jnp.where(cluster_of == c, fnbr[i : i + 1, :] - E * g, -1)
                cols = slice(i * E, (i + 1) * E)
                pick[c, g, :, cols] = jnp.where(element_rows == row, 1.0, 0.0).astype(BF16)

    derive(0, (0, 1, 2))
    for c in range(3):
        for r in range(REACH):
            for t in range(N_SUB):
                tab[c, r : r + 1, SLOT * t : SLOT * (t + 1)] = stab[c, r, t : t + 1, :]
    prepare_pick_send(0)
    pack(0, ROUTES[0, 0])

    @pl.loop(0, REACH)
    def _(r):
        peer = dom - r + 2

        @pl.when((peer < 0) | (peer >= n_dom))
        def _():
            @pl.loop(0, len(ROUTES))
            def _(route):
                for t in range(N_SUB):
                    recv[route, r * N_SUB + t] = jnp.zeros((PIECE, E), F32)

    groups = jnp.minimum(dom + 2, n_dom - 1) - jnp.maximum(dom - 2, 0) + 1
    pl.semaphore_wait(barrier, groups * N_SUB - 1)
    send_route(ROUTES[0, 0])

    own_columns((0, 1, 2))
    wide_at = 3
    for i in range(4):
        wide[wide_at + i, :FB, :B] = ftrace[i]
    a_tr[...] = jnp.concatenate(
        [weights(wide[wide_at + i, 0:16, :], KP) for i in range(4)], axis=0
    ).astype(BF16)
    wide_at += 4
    fer[...] = jnp.full(fer.shape, -1, jnp.int32)
    for g in range(4):
        fer[g : g + 1, NF * g : NF * (g + 1)] = felem[...]
    for g in range(4):
        spot = jnp.where(element_rows == fer[g : g + 1, :], 1.0, 0.0)
        pick_f[g] = spot.astype(BF16)
        pick_ft[g] = spot.T.astype(BF16)
    cfs[...] = jnp.zeros(cfs.shape, F32)
    cfs[0:Q, 0:NF] = fcoef[...]
    cfs[16:17, 0:NF] = (fface[...] + 1).astype(F32)
    high, low = halves(cfs[...])
    spread = dot(jnp.concatenate([high, low], axis=0).astype(BF16), pick_ft[0])
    cfe[...] = spread[0:32] + spread[32:64]
    near[...] = jnp.zeros(near.shape, F32)
    x_state[...] = jnp.zeros(x_state.shape, BF16)
    send_near(0)

    for c in (1, 2):
        prepare_pick_send(c)
        pack(c, ROUTES[0, c])

    for d in range(3):
        wide[wide_at + d, :B, :B] = stiff[d]
    for i in range(4):
        wide[wide_at + 3 + i, :B, :B] = lflux[i]
    a_vol[...] = jnp.concatenate(
        [weights(wide[wide_at + m], KP) for m in range(7)] + [jnp.zeros((8, E), F32)], axis=0
    ).astype(BF16)
    wide_at += 7
    volume()
    prepare_pick(0)
    for i in range(4):
        for j in range(4):
            wide[wide_at + 4 * i + j, :B, :B] = nflux[i, j]
        a_nf[i] = jnp.concatenate(
            [weights(wide[wide_at + 4 * i + j], KP) for j in range(4)], axis=0
        ).astype(BF16)
    wide_at += 16
    for i in range(4):
        wide[wide_at + i, :B, :FB] = flift[i]
    a_li[...] = jnp.concatenate(
        [weights(wide[wide_at + i], 16) for i in range(4)], axis=0
    ).astype(BF16)
    local_gather(0, True)
    fault(0)
    prepare_pick(1)
    ghost_gather(0, ROUTES[0, 0])
    send_route(ROUTES[0, 1])
    neighbours()

    local_gather(1, True)
    derive(1, (0,))
    pack(0, ROUTES[1, 0])
    send_route(ROUTES[1, 0])
    own_columns((0,))
    send_near(1)
    volume()
    local_gather(0, False)
    prepare_pick(2)
    ghost_gather(1, ROUTES[0, 1])
    fault(1)
    ghost_gather(0, ROUTES[1, 0])
    send_route(ROUTES[0, 2])
    neighbours()

    local_gather(2, True)
    derive(2, (0, 1))
    pack(0, ROUTES[2, 0])
    send_route(ROUTES[2, 0])
    own_columns((0, 1))
    send_near(2)
    pack(1, ROUTES[2, 1])
    volume()
    local_gather(0, False)
    ghost_gather(2, ROUTES[0, 2])
    fault(2)
    ghost_gather(0, ROUTES[2, 0])
    send_route(ROUTES[2, 1])
    neighbours()

    local_gather(1, True)
    derive(3, (0,))
    pack(0, ROUTES[3, 0])
    send_route(ROUTES[3, 0])
    own_columns((0,))
    send_near(3)
    volume()
    local_gather(0, False)
    ghost_gather(1, ROUTES[2, 1])
    fault(3)
    ghost_gather(0, ROUTES[3, 0])
    neighbours()
    out[...] = cur[:, :B, :]

    @pl.loop(0, len(ROUTES))
    def _(route):
        @pl.loop(0, PEERS)
        def _(idx):
            peer, t, valid = out_peer(idx)

            @pl.when(valid)
            def _():
                ghost_copy(route, idx, (idx // N_SUB) * N_SUB + sub, peer, t).wait_send()

    for s in range(4):
        far_copy(s).wait_send()


def body(n_dom, *args):
    args = list(args)
    for index in (4, 8, 9):
        args[index] = args[index].reshape(1, -1)
    routes = len(ROUTES)
    scratch = [
        pltpu.VMEM((Q, KP, E), F32),
        pltpu.VMEM((Q, KP, E), F32),
        pltpu.VMEM((3, Q, KP, E), F32),
        pltpu.VMEM((E, W), BF16),
        pltpu.VMEM((E, W), BF16),
        pltpu.VMEM((E, W), BF16),
        pltpu.VMEM((E, W), BF16),
        pltpu.VMEM((288, W), F32),
        pltpu.VMEM((4 * KP, W), F32),
        pltpu.VMEM((4 * KP, W), F32),
        pltpu.VMEM((4 * KP, W), F32),
        pltpu.VMEM((4 * KP, E), F32),
        pltpu.VMEM((4 * KP, E), F32),
        pltpu.VMEM((4, KP, E), F32),
        pltpu.VMEM((4, KP, E), F32),
        pltpu.VMEM((ROWS, E), F32),
        pltpu.VMEM((3, ROWS, 2 * E), BF16),
        pltpu.VMEM((ROWS, 4 * E), F32),
        pltpu.VMEM((ROWS, 2 * E), BF16),
        pltpu.VMEM((ROWS, REACH * E), F32),
        pltpu.VMEM((3, 1 + REACH, E, 4 * E), BF16),
        pltpu.VMEM((3, E, REACH * E), BF16),
        pltpu.VMEM((4, E, E), BF16),
        pltpu.VMEM((4, E, E), BF16),
        pltpu.VMEM((E, E), BF16),
        pltpu.VMEM((288, E), BF16),
        pltpu.VMEM((4, 4 * KP, E), BF16),
        pltpu.VMEM((64, E), BF16),
        pltpu.VMEM((4 * KP, E), BF16),
        pltpu.VMEM((34, KP, E), F32),
        pltpu.VMEM((3, 8, E), jnp.int32),
        pltpu.VMEM((8, E), jnp.int32),
        pltpu.VMEM((32, E), F32),
        pltpu.VMEM((32, E), F32),
        pltpu.VMEM((16, E), F32),
        pltpu.VMEM((routes, PEERS, PIECE, E), F32),
        pltpu.VMEM((routes, PEERS, PIECE, E), F32),
        pltpu.SemaphoreType.DMA((routes, PEERS)),
        pltpu.SemaphoreType.DMA((routes, PEERS)),
        pltpu.SemaphoreType.DMA((4,)),
        pltpu.SemaphoreType.DMA((4,)),
    ]
    return pl.pallas_call(
        functools.partial(kernel, n_dom),
        out_shape=jax.ShapeDtypeStruct((Q, B, E), F32),
        in_specs=[pl.BlockSpec(memory_space=pltpu.VMEM)] * len(args),
        out_specs=pl.BlockSpec(memory_space=pltpu.VMEM),
        scratch_shapes=scratch,
        compiler_params=pltpu.CompilerParams(
            collective_id=0, has_side_effects=True, vmem_limit_bytes=48 * 1024 * 1024
        ),
    )(*args)


def solution(mesh):
    in_specs = (
        P(None, None, ("dom", "sub")),
        P(None, None, None, ("dom", "sub")),
        P(None, None, None, ("dom", "sub")),
        P(None, None, None, ("dom", "sub")),
        P(("dom", "sub")),
        P(None, ("dom", "sub")),
        P(None, ("dom", "sub")),
        P(("dom", "sub"), None, None, None),
        P(("dom", "sub")),
        P(("dom", "sub")),
        P(None, ("dom", "sub")),
        P(),
        P(),
        P(),
        P(),
        P(),
        P(),
    )
    out_specs = P(None, None, ("dom", "sub"))
    return jax.shard_map(
        functools.partial(body, mesh.shape["dom"]),
        mesh=mesh,
        in_specs=in_specs,
        out_specs=out_specs,
        check_vma=False,
    )
```

time: 763 us -> 102 us (0.13)
  the two profiles are of different devices: /device:TPU:129 before, /device:TPU:178 now
where the time goes in v1:
time: 102 us; the launch traced here: 101 us
  Pallas kernels  94.7 us (93%)
  local copies, waits for them, and re-layouts  6.17 us (6%)
    pallas_call x1, Pallas kernels, body(): pl.pallas_call(functools.partial(kernel, n_dom), out_shape=jax.ShapeDtype...  94.7 us
    unnamed x38, local copies, waits for them, and re-layouts  6.17 us

profile of v1, /device:TPU:178, one launch (start us, length us, event | category | flops | bytes accessed | tf_op | source)
XLA Modules:
  0.0 101.0 jit_solution(134751421021278806)
XLA Ops:
  0.0 0.0 copy-start.13
  0.0 0.8 copy.23.ftrace
  0.8 0.0 copy-start.14
  0.8 0.9 copy.21.lflux
  1.7 0.0 copy-done.14
  1.7 0.1 copy.24.flift
  1.8 0.0 copy-done.13
  1.8 0.0 copy-start.11
  1.9 0.9 copy-done.11
  2.7 0.0 copy-start.12
  2.8 0.9 copy-done.12
  3.7 0.0 copy-start.10
  3.7 0.9 copy-done.10
  4.6 0.0 copy-start
  4.6 0.0 copy-start.1
  4.6 0.0 copy-start.2
  4.6 0.0 copy-start.3
  4.6 0.0 copy-start.4
  4.6 0.0 copy-start.5
  4.7 0.0 copy-start.6
  4.7 0.0 copy-start.7
  4.7 0.0 copy-start.8
  4.7 0.0 copy-start.9
  4.7 0.8 copy-done
  5.5 0.0 copy-done.1
  5.5 0.0 copy-done.2
  5.6 0.0 copy-done.3
  5.6 0.0 copy-done.4
  5.6 0.0 copy-done.5
  5.6 0.0 copy-done.6
  5.6 0.0 copy-done.7
  5.6 0.0 copy-done.8
  5.6 0.0 copy-done.9
  5.6 94.7 %shard_map.163 = f32[9,35,128]{2,1,0:T(8,128)S(1)} custom-call(f32[9,35,128]{2,1,0:T(8,128)S(1)} %copy-done, f32[3,9,9,128]{3,2,1,0:T(8,128)S(1)} %copy.18.star, f32[4,9,9,128]{3,2,1,0:T(8,128)S(1)} %copy.19.lsol, f32[4,9,9,128]{3,2,1,0:T(8,128)S(1)} %copy.20.nsol, s32[1,128]{1,0:T(1,128)S(1)} %bitcast.3, s32[4,128]{1,0:T(4,128)S(1)} %copy-done.5, ...), custom_call_target="tpu_custom_call" | custom-call | tf_op jit(solution)/shard_map/pallas_call | solution.py:584
  100.3 0.7 copy.26
  (4 shorter events, 0.1 us)
Async XLA Ops:
  0.0 1.8 %copy-start.13 = (f32[3,9,9,128]{3,0,2,1:T(4,128)S(1)}, f32[3,9,9,128]{3,0,2,1:T(4,128)}, u32[]{:S(2)}) copy-start(f32[3,9,9,128]{3,0,2,1:T(4,128)} %param.18) | copy-start | bytes 373252
  0.8 0.9 copy-start.14
  1.8 0.9 copy-start.11
  2.7 0.9 copy-start.12
  3.7 1.0 copy-start.10
  4.6 0.9 copy-start
  4.6 0.9 copy-start.1
  4.6 0.9 copy-start.2
  4.6 0.9 copy-start.3
  4.6 0.9 copy-start.4
  4.6 0.9 copy-start.5
  4.7 0.9 copy-start.6
  4.7 0.9 copy-start.7
  4.7 0.9 copy-start.8
  4.7 0.9 copy-start.9

commit v2 on v1

--- a/solution.py
+++ b/solution.py
@@ -65,6 +65,24 @@
 
 def kernel(
     n_dom,
+    dofs_hbm,
+    star_hbm,
+    lsol_hbm,
+    nsol_hbm,
+    ecl_hbm,
+    fnbr_hbm,
+    nface_hbm,
+    stab_hbm,
+    felem_hbm,
+    fface_hbm,
+    fcoef_hbm,
+    ck_hbm,
+    stiff_hbm,
+    lflux_hbm,
+    nflux_hbm,
+    ftrace_hbm,
+    flift_hbm,
+    out,
     dofs,
     star,
     lsol,
@@ -82,7 +100,6 @@
     nflux,
     ftrace,
     flift,
-    out,
     base,
     cur,
     integ,
@@ -113,6 +130,7 @@
     a_tr,
     a_li,
     wide,
+    sides_in,
     tab,
     fer,
     cfs,
@@ -124,6 +142,7 @@
     recv_sem,
     fsend_sem,
     frecv_sem,
+    load_sem,
 ):
     dom = lax.axis_index("dom")
     sub = lax.axis_index("sub")
@@ -140,6 +159,32 @@
         valid = (peer >= 0) & (peer < n_dom) & jnp.logical_not((r == 2) & (t == sub))
         return peer, t, valid
 
+    loads = [
+        pltpu.make_async_copy(source, target, load_sem.at[k])
+        for k, (source, target) in enumerate(
+            (
+                (dofs_hbm, dofs),
+                (ck_hbm, ck),
+                (ecl_hbm, ecl),
+                (star_hbm, star),
+                (stab_hbm, stab),
+                (felem_hbm, felem),
+                (fface_hbm, fface),
+                (fcoef_hbm, fcoef),
+                (ftrace_hbm, ftrace),
+                (stiff_hbm, stiff),
+                (lflux_hbm, lflux),
+                (lsol_hbm, lsol),
+                (fnbr_hbm, fnbr),
+                (nface_hbm, nface),
+                (flift_hbm, flift),
+                (nflux_hbm, nflux),
+                (nsol_hbm, nsol),
+            )
+        )
+    ]
+    for load in loads:
+        load.start()
     barrier = pltpu.get_barrier_semaphore()
 
     @pl.loop(0, PEERS)
@@ -155,6 +200,8 @@
     even = (lane // 32) % 2 == 0
     element_rows = lax.broadcasted_iota(jnp.int32, (E, E), 0)
 
+    for load in loads[:5]:
+        load.wait()
     base[...] = jnp.zeros((Q, KP, E), F32)
     base[:, :B, :] = dofs[...]
     cur[...] = base[...]
@@ -170,7 +217,7 @@
         for q in range(Q):
             value = moved[rows : rows + KP, q * E : (q + 1) * E]
             for pp in range(3):
-                term = coef[first, group * 3 + pp, q : q + 1, :] * value
+                term = coef[group * 3 + pp, q, first : first + 1, :] * value
                 if acc[pp] is None:
                     acc[pp] = term if sign > 0 else -term
                 else:
@@ -215,7 +262,7 @@
                     for c in due:
                         integ[c, p] = integ[c, p] + wt[pl.ds(5 * c + 1 + j, 1), :] * acc[pp]
 
-    def pack(c, route):
+    def pack(c, route, now=False):
         for q in range(Q):
             comp[32 * q : 32 * q + 32, :] = integ[c, q, 0:32, :]
         for q in range(Q):
@@ -234,6 +281,8 @@
                 ]
                 for t, part in enumerate(exchanged(parts, low_half, even)):
                     send[route, r * N_SUB + t, 16 * chunk : 16 * chunk + 16, :] = part
+            if now:
+                send_block(route, r)
 
         recv[route, 2 * N_SUB + sub] = send[route, 2 * N_SUB + sub]
 
@@ -247,14 +296,14 @@
             device_id_type=MESH,
         )
 
-    def send_route(route):
-        @pl.loop(0, PEERS)
-        def _(idx):
-            peer, t, valid = out_peer(idx)
+    def send_block(route, r):
+        for t in range(N_SUB):
+            idx = r * N_SUB + t
+            peer, _, valid = out_peer(idx)
 
             @pl.when(valid)
             def _():
-                ghost_copy(route, idx, (idx // N_SUB) * N_SUB + sub, peer, t).start()
+                ghost_copy(route, idx, r * N_SUB + sub, peer, t).start()
 
     def local_gather(c, first):
         picks = pick[c, 0]
@@ -264,7 +313,10 @@
         else:
             got[...] += value
 
-    def ghost_gather(c, route):
+    def ghost_gather(c, route, then=None):
+        if then is not None:
+            for r in range(1):
+                send_block(then, r)
         @pl.loop(0, REACH)
         def _(r):
             for t in range(N_SUB):
@@ -274,6 +326,12 @@
                 @pl.when(valid)
                 def _():
                     ghost_copy(route, idx, idx, peer, t).wait_recv()
+
+            if then is not None:
+
+                @pl.when(r + 1 < REACH)
+                def _():
+                    send_block(then, r + 1)
 
             for chunk in range(PIECE // 16):
                 parts = [
@@ -377,7 +435,7 @@
                 for q in range(Q):
                     value = lifted[i * KP : (i + 1) * KP, q * E : (q + 1) * E]
                     for pp in range(3):
-                        acc[pp] = acc[pp] - nsol[i, group * 3 + pp, q : q + 1, :] * value
+                        acc[pp] = acc[pp] - nsol[group * 3 + pp, q, i : i + 1, :] * value
             for pp in range(3):
                 cur[group * 3 + pp] = acc[pp]
 
@@ -400,8 +458,6 @@
             for t in range(N_SUB):
                 tab[c, r : r + 1, SLOT * t : SLOT * (t + 1)] = stab[c, r, t : t + 1, :]
     prepare_pick_send(0)
-    pack(0, ROUTES[0, 0])
-
     @pl.loop(0, REACH)
     def _(r):
         peer = dom - r + 2
@@ -415,12 +471,16 @@
 
     groups = jnp.minimum(dom + 2, n_dom - 1) - jnp.maximum(dom - 2, 0) + 1
     pl.semaphore_wait(barrier, groups * N_SUB - 1)
-    send_route(ROUTES[0, 0])
-
+
+    pack(0, ROUTES[0, 0], True)
+
+
+    for load in loads[5:9]:
+        load.wait()
     own_columns((0, 1, 2))
     wide_at = 3
     for i in range(4):
-        wide[wide_at + i, :FB, :B] = ftrace[i]
+        wide[wide_at + i, :FB, :B] = ftrace[:, i, :]
     a_tr[...] = jnp.concatenate(
         [weights(wide[wide_at + i, 0:16, :], KP) for i in range(4)], axis=0
     ).astype(BF16)
@@ -446,10 +506,12 @@
         prepare_pick_send(c)
         pack(c, ROUTES[0, c])
 
+    for load in loads[9:]:
+        load.wait()
     for d in range(3):
         wide[wide_at + d, :B, :B] = stiff[d]
     for i in range(4):
-        wide[wide_at + 3 + i, :B, :B] = lflux[i]
+        wide[wide_at + 3 + i, :B, :B] = lflux[:, i, :]
     a_vol[...] = jnp.concatenate(
         [weights(wide[wide_at + m], KP) for m in range(7)] + [jnp.zeros((8, E), F32)], axis=0
     ).astype(BF16)
@@ -458,27 +520,27 @@
     prepare_pick(0)
     for i in range(4):
         for j in range(4):
-            wide[wide_at + 4 * i + j, :B, :B] = nflux[i, j]
+            wide[wide_at + 4 * i + j, :B, :B] = nflux[i, :, j, :]
         a_nf[i] = jnp.concatenate(
             [weights(wide[wide_at + 4 * i + j], KP) for j in range(4)], axis=0
         ).astype(BF16)
     wide_at += 16
+    sides_in[...] = jnp.zeros((E, E), F32)
     for i in range(4):
-        wide[wide_at + i, :B, :FB] = flift[i]
-    a_li[...] = jnp.concatenate(
-        [weights(wide[wide_at + i], 16) for i in range(4)], axis=0
-    ).astype(BF16)
+        sides_in[16 * i : 16 * i + FB, :B] = flift[:, i, :]
+    sides = sides_in[...].T[0:KP]
+    first = lax.broadcasted_iota(jnp.int32, (KP, E), 1) < 16
+    parts = [jnp.where(first, pltpu.roll(sides, (E - 16 * i) % E, 1), 0.0) for i in range(4)]
+    a_li[...] = jnp.concatenate([weights(part, 16) for part in parts], axis=0).astype(BF16)
     local_gather(0, True)
     fault(0)
     prepare_pick(1)
-    ghost_gather(0, ROUTES[0, 0])
-    send_route(ROUTES[0, 1])
+    ghost_gather(0, ROUTES[0, 0], ROUTES[0, 1])
     neighbours()
 
     local_gather(1, True)
     derive(1, (0,))
-    pack(0, ROUTES[1, 0])
-    send_route(ROUTES[1, 0])
+    pack(0, ROUTES[1, 0], True)
     own_columns((0,))
     send_near(1)
     volume()
@@ -486,14 +548,12 @@
     prepare_pick(2)
     ghost_gather(1, ROUTES[0, 1])
     fault(1)
-    ghost_gather(0, ROUTES[1, 0])
-    send_route(ROUTES[0, 2])
+    ghost_gather(0, ROUTES[1, 0], ROUTES[0, 2])
     neighbours()
 
     local_gather(2, True)
     derive(2, (0, 1))
-    pack(0, ROUTES[2, 0])
-    send_route(ROUTES[2, 0])
+    pack(0, ROUTES[2, 0], True)
     own_columns((0, 1))
     send_near(2)
     pack(1, ROUTES[2, 1])
@@ -501,14 +561,12 @@
     local_gather(0, False)
     ghost_gather(2, ROUTES[0, 2])
     fault(2)
-    ghost_gather(0, ROUTES[2, 0])
-    send_route(ROUTES[2, 1])
+    ghost_gather(0, ROUTES[2, 0], ROUTES[2, 1])
     neighbours()
 
     local_gather(1, True)
     derive(3, (0,))
-    pack(0, ROUTES[3, 0])
-    send_route(ROUTES[3, 0])
+    pack(0, ROUTES[3, 0], True)
     own_columns((0,))
     send_near(3)
     volume()
@@ -537,8 +595,13 @@
     args = list(args)
     for index in (4, 8, 9):
         args[index] = args[index].reshape(1, -1)
+    for index, order in ((1, (1, 2, 0, 3)), (2, (1, 2, 0, 3)), (3, (1, 2, 0, 3))):
+        args[index] = args[index].transpose(order)
+    for index, order in ((13, (1, 0, 2)), (14, (0, 2, 1, 3)), (15, (1, 0, 2)), (16, (2, 0, 1))):
+        args[index] = args[index].transpose(order)
+    specs = [pl.BlockSpec(memory_space=pltpu.HBM)] * len(args)
     routes = len(ROUTES)
-    scratch = [
+    scratch = [pltpu.VMEM(arg.shape, arg.dtype) for arg in args] + [
         pltpu.VMEM((Q, KP, E), F32),
         pltpu.VMEM((Q, KP, E), F32),
         pltpu.VMEM((3, Q, KP, E), F32),
@@ -568,7 +631,8 @@
         pltpu.VMEM((4, 4 * KP, E), BF16),
         pltpu.VMEM((64, E), BF16),
         pltpu.VMEM((4 * KP, E), BF16),
-        pltpu.VMEM((34, KP, E), F32),
+        pltpu.VMEM((30, KP, E), F32),
+        pltpu.VMEM((E, E), F32),
         pltpu.VMEM((3, 8, E), jnp.int32),
         pltpu.VMEM((8, E), jnp.int32),
         pltpu.VMEM((32, E), F32),
@@ -580,15 +644,16 @@
         pltpu.SemaphoreType.DMA((routes, PEERS)),
         pltpu.SemaphoreType.DMA((4,)),
         pltpu.SemaphoreType.DMA((4,)),
+        pltpu.SemaphoreType.DMA((17,)),
     ]
     return pl.pallas_call(
         functools.partial(kernel, n_dom),
         out_shape=jax.ShapeDtypeStruct((Q, B, E), F32),
-        in_specs=[pl.BlockSpec(memory_space=pltpu.VMEM)] * len(args),
+        in_specs=specs,
         out_specs=pl.BlockSpec(memory_space=pltpu.VMEM),
         scratch_shapes=scratch,
         compiler_params=pltpu.CompilerParams(
-            collective_id=0, has_side_effects=True, vmem_limit_bytes=48 * 1024 * 1024
+            collective_id=0, has_side_effects=True, vmem_limit_bytes=60 * 1024 * 1024
         ),
     )(*args)
 

time: 102 us -> 91.9 us (0.901)
  Pallas kernels: 94.7 us -> 90 us
  local copies, waits for them, and re-layouts: 6.17 us -> 1.61 us
    pallas_call x1, Pallas kernels: 94.7 us -> 90 us  [body(): pl.pallas_call(functools.partial(kernel, n_dom), out_shape=jax.ShapeDtype...]
    unnamed x38 -> x1, local copies, waits for them, and re-layouts: 6.17 us -> 1.61 us
where the time goes in v2:
time: 91.9 us; the launch traced here: 91.6 us
  Pallas kernels  90 us (98%)
  local copies, waits for them, and re-layouts  1.61 us (2%)
    pallas_call x1, Pallas kernels, body(): pl.pallas_call(functools.partial(kernel, n_dom), out_shape=jax.ShapeDtype...  90 us

profile of v2, /device:TPU:178, one launch (start us, length us, event | category | flops | bytes accessed | tf_op | source)
XLA Modules:
  0.0 91.6 jit_solution(18382439866010507882)
XLA Ops:
  0.0 90.0 %shard_map.163 = f32[9,35,128]{2,1,0:T(8,128)} custom-call(f32[9,35,128]{2,1,0:T(8,128)} %dofs_hbm.1, f32[9,9,3,128]{3,2,1,0:T(4,128)} %bitcast.11, f32[9,9,4,128]{3,2,1,0:T(4,128)} %bitcast.12, f32[9,9,4,128]{3,2,1,0:T(4,128)} %bitcast.13, s32[1,128]{1,0:T(1,128)} %bitcast.17, s32[4,128]{1,0:T(4,128)} %fnbr_hbm.1, s32[4,128]{1,0:T(4,128)} %nface_hbm.1, ...), custom_call_target="tpu_custom_call" | custom-call | tf_op jit(solution)/shard_map/pallas_call | solution.py:649
  90.0 1.6 %copy.19 = f32[9,35,128]{2,1,0:T(8,128)} copy(f32[9,35,128]{2,1,0:T(8,128)} %shard_map.163) | data formatting | bytes 322560

commit v3 on v2

--- a/solution.py
+++ b/solution.py
@@ -305,6 +305,17 @@
             def _():
                 ghost_copy(route, idx, r * N_SUB + sub, peer, t).start()
 
+    def sent(*routes):
+        for route in routes:
+
+            @pl.loop(0, PEERS)
+            def _(idx, route=route):
+                peer, t, valid = out_peer(idx)
+
+                @pl.when(valid)
+                def _():
+                    ghost_copy(route, idx, (idx // N_SUB) * N_SUB + sub, peer, t).wait_send()
+
     def local_gather(c, first):
         picks = pick[c, 0]
         value = dot(comp_h[c], jnp.concatenate([picks, picks], axis=0))
@@ -385,8 +396,7 @@
     def volume():
         moved[...] = dot(a_vol[...], x_own[...])
 
-        @pl.loop(0, 3)
-        def _(group):
+        for group in range(3):
             acc = [cur[group * 3 + pp] for pp in range(3)]
             for d in range(3):
                 acc = star_terms(acc, star, d, d * KP, group, 1)
@@ -411,16 +421,15 @@
         lift[...] = dot(a_li[...], x_state[...])
 
     def neighbours():
-        @pl.loop(0, 4)
-        def _(i):
+        for i in range(4):
             for q in range(Q):
-                main = got[32 * q : 32 * q + 32, lanes(i)]
-                tail = got[TAIL + 3 * q : TAIL + 3 * q + 8, lanes(i)]
+                main = got[32 * q : 32 * q + 32, i * E : (i + 1) * E]
+                tail = got[TAIL + 3 * q : TAIL + 3 * q + 8, i * E : (i + 1) * E]
                 x_nbr[:, q * E : (q + 1) * E] = stacked(jnp.concatenate([main, tail], axis=0))
             across[...] = dot(a_nf[i], x_nbr[...])
-            which = nface[pl.ds(i, 1), :]
-            mark = cfe[16:17, :] == (i + 1).astype(F32)
-            at = pl.multiple_of(i * KP, 8)
+            which = nface[i : i + 1, :]
+            mark = cfe[16:17, :] == (i + 1.0)
+            at = i * KP
             for q in range(Q):
                 cols = slice(q * E, (q + 1) * E)
                 value = across[3 * KP : 4 * KP, cols]
@@ -428,8 +437,7 @@
                     value = jnp.where(which == j, across[j * KP : (j + 1) * KP, cols], value)
                 lifted[pl.ds(at, KP), cols] = value + jnp.where(mark, lift[pl.ds(at, KP), cols], 0.0)
 
-        @pl.loop(0, 3)
-        def _(group):
+        for group in range(3):
             acc = [cur[group * 3 + pp] for pp in range(3)]
             for i in range(4):
                 for q in range(Q):
@@ -538,9 +546,9 @@
     ghost_gather(0, ROUTES[0, 0], ROUTES[0, 1])
     neighbours()
 
-    local_gather(1, True)
     derive(1, (0,))
     pack(0, ROUTES[1, 0], True)
+    local_gather(1, True)
     own_columns((0,))
     send_near(1)
     volume()
@@ -548,12 +556,13 @@
     prepare_pick(2)
     ghost_gather(1, ROUTES[0, 1])
     fault(1)
+    sent(ROUTES[0, 0])
     ghost_gather(0, ROUTES[1, 0], ROUTES[0, 2])
     neighbours()
 
-    local_gather(2, True)
     derive(2, (0, 1))
     pack(0, ROUTES[2, 0], True)
+    local_gather(2, True)
     own_columns((0, 1))
     send_near(2)
     pack(1, ROUTES[2, 1])
@@ -561,32 +570,25 @@
     local_gather(0, False)
     ghost_gather(2, ROUTES[0, 2])
     fault(2)
+    sent(ROUTES[0, 1], ROUTES[1, 0])
     ghost_gather(0, ROUTES[2, 0], ROUTES[2, 1])
     neighbours()
 
-    local_gather(1, True)
     derive(3, (0,))
     pack(0, ROUTES[3, 0], True)
+    local_gather(1, True)
     own_columns((0,))
     send_near(3)
     volume()
     local_gather(0, False)
     ghost_gather(1, ROUTES[2, 1])
     fault(3)
+    sent(ROUTES[0, 2], ROUTES[2, 0], ROUTES[2, 1])
     ghost_gather(0, ROUTES[3, 0])
     neighbours()
     out[...] = cur[:, :B, :]
 
-    @pl.loop(0, len(ROUTES))
-    def _(route):
-        @pl.loop(0, PEERS)
-        def _(idx):
-            peer, t, valid = out_peer(idx)
-
-            @pl.when(valid)
-            def _():
-                ghost_copy(route, idx, (idx // N_SUB) * N_SUB + sub, peer, t).wait_send()
-
+    sent(ROUTES[3, 0])
     for s in range(4):
         far_copy(s).wait_send()
 

time: 91.9 us -> 91.9 us (level)
  no operation moved by 1% of the time
where the time goes in v3:
time: 91.9 us; the launch traced here: 91.8 us
  Pallas kernels  90.2 us (98%)
  local copies, waits for them, and re-layouts  1.61 us (2%)
    pallas_call x1, Pallas kernels, body(): pl.pallas_call(functools.partial(kernel, n_dom), out_shape=jax.ShapeDtype...  90.2 us

profile of v3, /device:TPU:178, one launch (start us, length us, event | category | flops | bytes accessed | tf_op | source)
XLA Modules:
  0.0 91.8 jit_solution(16916550947240938263)
XLA Ops:
  0.0 90.2 %shard_map.163 = f32[9,35,128]{2,1,0:T(8,128)} custom-call(f32[9,35,128]{2,1,0:T(8,128)} %dofs_hbm.1, f32[9,9,3,128]{3,2,1,0:T(4,128)} %bitcast.11, f32[9,9,4,128]{3,2,1,0:T(4,128)} %bitcast.12, f32[9,9,4,128]{3,2,1,0:T(4,128)} %bitcast.13, s32[1,128]{1,0:T(1,128)} %bitcast.17, s32[4,128]{1,0:T(4,128)} %fnbr_hbm.1, s32[4,128]{1,0:T(4,128)} %nface_hbm.1, ...), custom_call_target="tpu_custom_call" | custom-call | tf_op jit(solution)/shard_map/pallas_call | solution.py:651
  90.2 1.6 %copy.19 = f32[9,35,128]{2,1,0:T(8,128)} copy(f32[9,35,128]{2,1,0:T(8,128)} %shard_map.163) | data formatting | bytes 322560

commit v4 on v3

--- a/solution.py
+++ b/solution.py
@@ -297,7 +297,8 @@
         )
 
     def send_block(route, r):
-        for t in range(N_SUB):
+        for turn in (2, 1, 3, 0):
+            t = (sub + turn) % N_SUB
             idx = r * N_SUB + t
             peer, _, valid = out_peer(idx)
 

time: 91.9 us -> 90.5 us (0.985); the launches traced: 91.8 us -> 89.3 us
  Pallas kernels: 90.2 us -> 87.7 us
    pallas_call x1, Pallas kernels: 90.2 us -> 87.7 us  [body(): pl.pallas_call(functools.partial(kernel, n_dom), out_shape=jax.ShapeDtype...]
where the time goes in v4:
time: 90.5 us; the launch traced here: 89.3 us
  Pallas kernels  87.7 us (97%)
  local copies, waits for them, and re-layouts  1.61 us (2%)
    pallas_call x1, Pallas kernels, body(): pl.pallas_call(functools.partial(kernel, n_dom), out_shape=jax.ShapeDtype...  87.7 us

profile of v4, /device:TPU:178, one launch (start us, length us, event | category | flops | bytes accessed | tf_op | source)
XLA Modules:
  0.0 89.3 jit_solution(17108428231249811694)
XLA Ops:
  0.0 87.7 %shard_map.163 = f32[9,35,128]{2,1,0:T(8,128)} custom-call(f32[9,35,128]{2,1,0:T(8,128)} %dofs_hbm.1, f32[9,9,3,128]{3,2,1,0:T(4,128)} %bitcast.11, f32[9,9,4,128]{3,2,1,0:T(4,128)} %bitcast.12, f32[9,9,4,128]{3,2,1,0:T(4,128)} %bitcast.13, s32[1,128]{1,0:T(1,128)} %bitcast.17, s32[4,128]{1,0:T(4,128)} %fnbr_hbm.1, s32[4,128]{1,0:T(4,128)} %nface_hbm.1, ...), custom_call_target="tpu_custom_call" | custom-call | tf_op jit(solution)/shard_map/pallas_call | solution.py:652
  87.7 1.6 %copy.19 = f32[9,35,128]{2,1,0:T(8,128)} copy(f32[9,35,128]{2,1,0:T(8,128)} %shard_map.163) | data formatting | bytes 322560

commit v5 on v4

--- a/solution.py
+++ b/solution.py
@@ -273,7 +273,8 @@
         packed[...] = dot(comp_h[c], jnp.concatenate([picks, picks], axis=0))
 
         @pl.loop(0, REACH)
-        def _(r):
+        def _(b):
+            r = turned(b)
             for chunk in range(PIECE // 16):
                 parts = [
                     packed[PIECE * g + 16 * chunk : PIECE * g + 16 * chunk + 16, lanes(r)]
@@ -286,6 +287,10 @@
 
         recv[route, 2 * N_SUB + sub] = send[route, 2 * N_SUB + sub]
 
+    def turned(b):
+        near_first = REACH - 1 - b
+        return jnp.where(near_first % 2 == 0, near_first // 2, REACH - 1 - near_first // 2)
+
     def ghost_copy(route, out_idx, landing, peer, t):
         return pltpu.make_async_remote_copy(
             src_ref=send.at[route, out_idx],
@@ -327,10 +332,10 @@
 
     def ghost_gather(c, route, then=None):
         if then is not None:
-            for r in range(1):
-                send_block(then, r)
+            send_block(then, 2)
         @pl.loop(0, REACH)
-        def _(r):
+        def _(b):
+            r = turned(b)
             for t in range(N_SUB):
                 idx = r * N_SUB + t
                 peer, _, valid = in_peer(idx)
@@ -341,9 +346,9 @@
 
             if then is not None:
 
-                @pl.when(r + 1 < REACH)
+                @pl.when(b + 1 < REACH)
                 def _():
-                    send_block(then, r + 1)
+                    send_block(then, turned(b + 1))
 
             for chunk in range(PIECE // 16):
                 parts = [

time: 90.5 us -> 91.1 us (level)
  the two profiles are of different devices: /device:TPU:178 before, /device:TPU:229 now
where the time goes in v5:
time: 91.1 us; the launch traced here: 91 us
  Pallas kernels  89.4 us (98%)
  local copies, waits for them, and re-layouts  1.61 us (2%)
    pallas_call x1, Pallas kernels, body(): pl.pallas_call(functools.partial(kernel, n_dom), out_shape=jax.ShapeDtype...  89.4 us

profile of v5, /device:TPU:229, one launch (start us, length us, event | category | flops | bytes accessed | tf_op | source)
XLA Modules:
  0.0 91.0 jit_solution(11690798839970488376)
XLA Ops:
  0.0 89.4 %shard_map.163 = f32[9,35,128]{2,1,0:T(8,128)} custom-call(f32[9,35,128]{2,1,0:T(8,128)} %dofs_hbm.1, f32[9,9,3,128]{3,2,1,0:T(4,128)} %bitcast.11, f32[9,9,4,128]{3,2,1,0:T(4,128)} %bitcast.12, f32[9,9,4,128]{3,2,1,0:T(4,128)} %bitcast.13, s32[1,128]{1,0:T(1,128)} %bitcast.17, s32[4,128]{1,0:T(4,128)} %fnbr_hbm.1, s32[4,128]{1,0:T(4,128)} %nface_hbm.1, ...), custom_call_target="tpu_custom_call" | custom-call | tf_op jit(solution)/shard_map/pallas_call | solution.py:657
  89.4 1.6 %copy.19 = f32[9,35,128]{2,1,0:T(8,128)} copy(f32[9,35,128]{2,1,0:T(8,128)} %shard_map.163) | data formatting | bytes 322560
